TPU v7x, 256 devices: a whole 4x4x8 slice. The times are simulated.
256 devices in a mesh: rep: 2 (over core), own: 128 (over z, x, y).
Axes of the slice: x: 4, y: 4, z: 8, core: 2. Of those that a mesh axis runs over, the one named last changes fastest.
Arguments:
- embeddings: bfloat16 [65536, 1024], P(('rep', 'own'))
- cluster: int32 [65536], P(('rep', 'own')), may hold values from 0 to 511, as said below
- order: int32 [65536], P(('rep', 'own')), may hold values from 0 to 65535, each once
Outputs:
- nearest: float32 [65536], P(('rep', 'own'))
Inputs may be any that keep to these rules, and one draw needn't show every extreme that they name: `cluster`: cluster c belongs to owner c // 4. In each aligned block of 256 rows (the rows of one device) at most 4 rows name clusters of one owner; in every block exactly 4 rows name clusters of one owner that is the same for all blocks. `order`: Distinct.
All inputs are finite; a program needn't handle non-finite values.
Results may differ from a plain program's by a relative error of at most 0.0005.
Values may be sent and summed in bfloat16 or wider, within the bound.
A program may use at most 64 MiB of HBM per device.

v0:
```python
import jax
import jax.numpy as jnp
from jax import lax
from jax.sharding import PartitionSpec as P

CL_DEV = 4


def best_against(current, query_unit, query_cluster, query_order, key_unit, key_cluster, key_order):
    count = key_unit.shape[0]
    group = 512
    parts = count // group
    grouped_unit = key_unit.reshape(parts, group, key_unit.shape[1])
    grouped_cluster = key_cluster.reshape(parts, group)
    grouped_order = key_order.reshape(parts, group)

    def step_keys(running, pieces):
        block_unit, block_cluster, block_order = pieces
        similar = lax.dot_general(
            query_unit, block_unit, (((1,), (1,)), ((), ())), preferred_element_type=jnp.float32
        )
        allowed = (block_cluster[None, :] == query_cluster[:, None]) & (
            block_order[None, :] < query_order[:, None]
        )
        return (jnp.maximum(running, jnp.max(jnp.where(allowed, similar, -1.0), axis=1)), None)

    result, unused = lax.scan(step_keys, current, (grouped_unit, grouped_cluster, grouped_order))
    return result


def body(embeddings, cluster, order):
    owners = lax.axis_size("own")
    local_rows = embeddings.shape[0]
    width_dim = embeddings.shape[1]
    capacity = 2 * local_rows // owners
    values = embeddings.astype(jnp.float32)
    scale = lax.rsqrt(jnp.sum(values * values, axis=-1, keepdims=True) + 1e-06)
    unit_rows = (values * scale).astype(jnp.bfloat16)
    dest_owner = cluster // CL_DEV
    one_hot = (dest_owner[:, None] == jnp.arange(owners, dtype=jnp.int32)[None, :]).astype(
        jnp.int32
    )
    slot_index = jnp.sum((jnp.cumsum(one_hot, axis=0) - 1) * one_hot, axis=1)
    placed = dest_owner * capacity + slot_index
    send_unit = (
        jnp.zeros((owners * capacity, width_dim), jnp.bfloat16)
        .at[placed]
        .set(unit_rows)
        .reshape(owners, capacity, width_dim)
    )
    send_cluster = (
        jnp.full((owners * capacity,), -1, jnp.int32)
        .at[placed]
        .set(cluster)
        .reshape(owners, capacity)
    )
    send_order = (
        jnp.zeros((owners * capacity,), jnp.int32).at[placed].set(order).reshape(owners, capacity)
    )
    got_unit, got_cluster, got_order = (
        lax.all_to_all(send_unit, "own", split_axis=0, concat_axis=0, tiled=True),
        lax.all_to_all(send_cluster, "own", split_axis=0, concat_axis=0, tiled=True),
        lax.all_to_all(send_order, "own", split_axis=0, concat_axis=0, tiled=True),
    )
    query_unit = got_unit.reshape(owners * capacity, width_dim)
    query_cluster = got_cluster.reshape(-1)
    query_order = got_order.reshape(-1)
    initial = jnp.full((owners * capacity,), -1.0, jnp.float32)
    best_rows = best_against(
        initial,
        query_unit,
        query_cluster,
        query_order,
        lax.all_gather(query_unit, "rep", axis=0, tiled=True),
        lax.all_gather(query_cluster, "rep", axis=0, tiled=True),
        lax.all_gather(query_order, "rep", axis=0, tiled=True),
    )
    home_best = lax.all_to_all(
        best_rows.reshape(owners, capacity), "own", split_axis=0, concat_axis=0, tiled=True
    ).reshape(-1)
    return home_best[placed]


def solution(mesh):
    placed = (P(("rep", "own"), None), P(("rep", "own")), P(("rep", "own")))
    return jax.shard_map(
        body, mesh=mesh, in_specs=placed, out_specs=P(("rep", "own")), check_vma=False
    )
```

profile of v0, /device:TPU:1, one launch (start us, length us, event | category | flops | bytes accessed | tf_op | source)
XLA Modules:
  0.0 137.1 jit_solution(2790143301987667064)
XLA Ops:
  6.5 0.7 fusion.20
  7.2 0.7 and_select_fusion
  8.0 0.2 fusion.11
  8.4 0.2 fusion.12
  8.5 0.7 compare_select_fusion
  9.2 1.2 fusion.5
  10.5 2.5 %scatter_custom_fusion.2 = bf16[512,1024]{1,0:T(8,128)(2,1)S(1)} fusion(s32[256]{0:T(256)S(1)} %compare_select_fusion, bf16[256,1024]{1,0:T(8,128)(2,1)} %param.5, f32[256]{0:T(256)S(1)} %add_rsqrt_fusion, bf16[]{:T(256)} %constant.43.clone.1), kind=kCustom, calls=%fused_computation.17 | custom fusion | flops 786432 | bytes 1573890 | tf_op jit(solution)/shard_map/scatter | solution.py:48
  13.0 0.4 reshape.70
  13.4 44.7 %all_to_all.38 = bf16[128,4,1024]{2,1,0:T(4,128)(2,1)S(1)} all-to-all(bf16[128,4,1024]{2,1,0:T(4,128)(2,1)S(1)} %reshape.70), channel_id=1, replica_groups=mesh['rep'=2,'own'=128] {'own'}, dimensions={0} | all-to-all | bytes 2097152 | tf_op jit(solution)/shard_map/all_to_all | solution.py:61
  58.1 1.1 reshape.71
  59.3 1.6 %scatter_custom_fusion.1 = s32[512]{0:T(512)S(1)} fusion(s32[256]{0:T(256)S(1)} %compare_select_fusion, s32[256]{0:T(256)} %param.7, s32[]{:T(128)} %constant.28.clone.1), kind=kCustom, calls=%fused_computation.38 | custom fusion | bytes 2560 | tf_op jit(solution)/shard_map/scatter | solution.py:58
  60.8 0.7 all_to_all.28
  61.6 8.0 %all-to-all-start.1 = ((s32[128,1,4]{2,1,0:T(1,128)}), s32[128,1,4]{2,1,0:T(1,128)S(1)}, u32[]{:S(2)}, u32[]{:S(2)}) async-start(s32[128,1,4]{2,1,0:T(1,128)} %bitcast.6), calls=%async_computation.1 | async-start | bytes 131072 | tf_op jit(solution)/shard_map/all_to_all | solution.py:63
  69.6 1.6 %scatter_custom_fusion = s32[512]{0:T(512)S(1)} fusion(s32[256]{0:T(256)S(1)} %compare_select_fusion, s32[256]{0:T(256)} %param.6, s32[]{:T(128)} %constant.47.clone.1), kind=kCustom, calls=%fused_computation.40 | custom fusion | bytes 2560 | tf_op jit(solution)/shard_map/scatter | solution.py:54
  71.2 0.7 all_to_all.25
  71.9 8.4 %all-to-all-done.1 = s32[128,1,4]{2,1,0:T(1,128)S(1)} async-done(((s32[128,1,4]{2,1,0:T(1,128)}), s32[128,1,4]{2,1,0:T(1,128)S(1)}, u32[]{:S(2)}, u32[]{:S(2)}) %all-to-all-start.1) | async-done | bytes 2080 | tf_op jit(solution)/shard_map/all_to_all | solution.py:63
  80.3 6.1 %all-to-all-start = ((s32[128,1,4]{2,1,0:T(1,128)}), s32[128,1,4]{2,1,0:T(1,128)S(1)}, u32[]{:S(2)}, u32[]{:S(2)}) async-start(s32[128,1,4]{2,1,0:T(1,128)} %bitcast.4), calls=%async_computation | async-start | bytes 131072 | tf_op jit(solution)/shard_map/all_to_all | solution.py:62
  86.4 0.5 broadcast.72
  86.9 0.7 reduce.10
  87.8 4.3 %all-gather.1 = s32[2,1,512]{2,1,0:T(1,128)S(1)} all-gather(s32[1,1,512]{2,1,0:T(1,128)S(1)} %reshape.112), channel_id=1, replica_groups=mesh['rep'=2,'own'=128] {'rep'}, dimensions={0}, use_global_device_ids=true | all-gather | bytes 6144 | tf_op jit(solution)/shard_map/all_gather | solution.py:76
  92.1 5.1 %all-to-all-done = s32[128,1,4]{2,1,0:T(1,128)S(1)} async-done(((s32[128,1,4]{2,1,0:T(1,128)}), s32[128,1,4]{2,1,0:T(1,128)S(1)}, u32[]{:S(2)}, u32[]{:S(2)}) %all-to-all-start) | async-done | bytes 2080 | tf_op jit(solution)/shard_map/all_to_all | solution.py:62
  97.1 0.7 reduce.9
  98.0 5.6 %all-gather = s32[2,1,512]{2,1,0:T(1,128)S(1)} all-gather(s32[1,1,512]{2,1,0:T(1,128)S(1)} %reshape.110), channel_id=1, replica_groups=mesh['rep'=2,'own'=128] {'rep'}, dimensions={0}, use_global_device_ids=true | all-gather | bytes 6144 | tf_op jit(solution)/shard_map/all_gather | solution.py:75
  103.9 4.8 %while.12 = (s32[]{:T(128)}, f32[512]{0:T(512)S(1)}, s32[2,512]{1,0:T(2,128)S(1)}, s32[128,4]{1,0:T(8,128)}, s32[2,512]{1,0:T(2,128)S(1)}, /*index=5*/s32[128,4]...) while((s32[]{:T(128)}, f32[512]{0:T(512)S(1)}, ...), condition=%wide.wide.region_9.10_spmd.clone, body=%wide.wide.region_7.9_spmd.clone.sunk | while | flops 538182144 | bytes 2122371 | solution.py:27
  103.9 2.3 %fusion.29 = f32[512]{0:T(512)S(1)} fusion(bf16[512,1024]{1,0:T(8,128)(2,1)} %get-tuple-element.222, bf16[2,512,1024]{2,1,0:T(8,128)(2,1)} %get-tuple-element.221, s32[]{:T(128)} %get-tuple-element.203, s32[512]{0:T(512)S(1)} %get-tuple-element.223, s32[512]{0:T(512)S(1)} %get-tuple-element.224, s32[512]{0:T(512)S(1)} %bitcast.53, ...), kind=kOutput, calls=%fused_computation.6.clone.clone.1 | convolution fusion | flops 538181120 | bytes 2107904 | tf_op jit(solution)/shard_map/while/body/eval_jaxpr/dot_general | solution.py:19
  106.3 2.3 %fusion.29 = f32[512]{0:T(512)S(1)} fusion(bf16[512,1024]{1,0:T(8,128)(2,1)} %get-tuple-element.222, bf16[2,512,1024]{2,1,0:T(8,128)(2,1)} %get-tuple-element.221, s32[]{:T(128)} %get-tuple-element.203, s32[512]{0:T(512)S(1)} %get-tuple-element.223, s32[512]{0:T(512)S(1)} %get-tuple-element.224, s32[512]{0:T(512)S(1)} %bitcast.53, ...), kind=kOutput, calls=%fused_computation.6.clone.clone.1 | convolution fusion | flops 538181120 | bytes 2107904 | tf_op jit(solution)/shard_map/while/body/eval_jaxpr/dot_general | solution.py:19
  108.7 0.7 all_to_all.32
  109.4 6.2 %all-to-all-start.3 = ((f32[128,1,4]{2,1,0:T(1,128)}), f32[128,1,4]{2,1,0:T(1,128)S(1)}, u32[]{:S(2)}, u32[]{:S(2)}) async-start(f32[128,1,4]{2,1,0:T(1,128)} %bitcast.9), calls=%async_computation.3 | async-start | bytes 131072 | tf_op jit(solution)/shard_map/all_to_all | solution.py:78
  115.6 10.7 %all-to-all-done.3 = f32[128,1,4]{2,1,0:T(1,128)S(1)} async-done(((f32[128,1,4]{2,1,0:T(1,128)}), f32[128,1,4]{2,1,0:T(1,128)S(1)}, u32[]{:S(2)}, u32[]{:S(2)}) %all-to-all-start.3) | async-done | bytes 2080 | tf_op jit(solution)/shard_map/all_to_all | solution.py:78
  126.3 0.5 broadcast.74
  126.8 0.8 reduce.11
  127.7 2.5 %gather_fusion = f32[256]{0:T(256)} fusion(f32[512]{0:T(512)S(1)} %reshape.73, s32[1024]{0:T(1024)S(1)} %pad_clamp_fusion), kind=kCustom, calls=%fused_computation | custom fusion | bytes 3072 | tf_op jit(solution)/shard_map/gather | solution.py:81
  (27 shorter events, 0.9 us)
Async XLA Ops:
  6.5 97.3 %all-gather.4.cloned.1.call-start = ((), (), s32[]{:S(2)}) async-start(), calls=%async_computation.4 | async-start | bytes 3145728 | tf_op jit(solution)/shard_map/all_gather | solution.py:74
  61.6 18.8 %all-to-all-start.1 = ((s32[128,1,4]{2,1,0:T(1,128)}), s32[128,1,4]{2,1,0:T(1,128)S(1)}, u32[]{:S(2)}, u32[]{:S(2)}) async-start(s32[128,1,4]{2,1,0:T(1,128)} %bitcast.6), calls=%async_computation.1 | async-start | bytes 131072 | tf_op jit(solution)/shard_map/all_to_all | solution.py:63
  80.3 23.5 %copy-start = (s32[128,1,4]{2,1,0:T(1,128)}, s32[128,1,4]{2,1,0:T(1,128)S(1)}, u32[]{:S(2)}) copy-start(s32[128,1,4]{2,1,0:T(1,128)S(1)} %all-to-all-done.1) | copy-start | bytes 6148
  80.3 16.8 %all-to-all-start = ((s32[128,1,4]{2,1,0:T(1,128)}), s32[128,1,4]{2,1,0:T(1,128)S(1)}, u32[]{:S(2)}, u32[]{:S(2)}) async-start(s32[128,1,4]{2,1,0:T(1,128)} %bitcast.4), calls=%async_computation | async-start | bytes 131072 | tf_op jit(solution)/shard_map/all_to_all | solution.py:62
  97.1 6.7 %copy-start.1 = (s32[128,1,4]{2,1,0:T(1,128)}, s32[128,1,4]{2,1,0:T(1,128)S(1)}, u32[]{:S(2)}) copy-start(s32[128,1,4]{2,1,0:T(1,128)S(1)} %all-to-all-done) | copy-start | bytes 6148
  109.4 16.9 %all-to-all-start.3 = ((f32[128,1,4]{2,1,0:T(1,128)}), f32[128,1,4]{2,1,0:T(1,128)S(1)}, u32[]{:S(2)}, u32[]{:S(2)}) async-start(f32[128,1,4]{2,1,0:T(1,128)} %bitcast.9), calls=%async_computation.3 | async-start | bytes 131072 | tf_op jit(solution)/shard_map/all_to_all | solution.py:78
Sparse Core Ops, SparseCore 0:
  59.4 12.8 all-gather.3
where the time goes:
time: 138 us; the launch traced here: 137 us
  blocking collectives  54.7 us (40%)
  waiting for transfers between devices  24.3 us (18%)
  starting transfers between devices  20.3 us (15%)
  between operations  13.6 us (10%)
  local copies, waits for them, and re-layouts  11 us (8%)
  other arithmetic  8.54 us (6%)
  matrix products  4.67 us (3%)
    all_to_all x1, blocking collectives, body(): lax.all_to_all(send_unit, 'own', split_axis=0, concat_axis=0, tiled=True)  44.7 us
    all_to_all x1, waiting for transfers between devices, body(): lax.all_to_all(best_rows.reshape(owners, capacity), 'own', split_axis=0,...  10.7 us
    all_to_all x1, waiting for transfers between devices, body(): lax.all_to_all(send_order, 'own', split_axis=0, concat_axis=0, tiled=True)  8.43 us
    all_to_all x1, starting transfers between devices, body(): lax.all_to_all(send_order, 'own', split_axis=0, concat_axis=0, tiled=True)  8.03 us
    all_to_all x1, starting transfers between devices, body(): lax.all_to_all(best_rows.reshape(owners, capacity), 'own', split_axis=0,...  6.17 us
    all_to_all x1, starting transfers between devices, body(): lax.all_to_all(send_cluster, 'own', split_axis=0, concat_axis=0, tiled=True)  6.07 us
    all_gather x1, blocking collectives, body(): lax.all_gather(query_cluster, 'rep', axis=0, tiled=True)  5.63 us
    all_to_all x1, waiting for transfers between devices, body(): lax.all_to_all(send_cluster, 'own', split_axis=0, concat_axis=0, tiled=True)  5.07 us
  transfers between devices with their start and end apart: 4, of which 3 were waited for; matrix products, arithmetic and copies ran while one was open for 4% of the time, Pallas kernels for 0%

commit v1 on v0

v1 whole, which is shorter than its diff:
```python
import jax
import jax.numpy as jnp
from jax import lax
from jax.experimental import pallas as pl
from jax.experimental.pallas import tpu as pltpu
from jax.sharding import PartitionSpec as P

MESH = pl.DeviceIdType.MESH
CL_DEV = 4
CAP = 4
NZ, NX, NY = 8, 4, 4
OWN = NZ * NX * NY
PLANE = NX * NY
ROWS = 256
D = 1024
SLOTS = OWN * CAP
WIDE = D // 4
MSG = 16
GROUP = PLANE * MSG
Z_ORDER = (4, 3, 5, 2, 6, 1, 7, 0)


def peer_of(me, dz, dx, dy):
    z, x, y = me // PLANE, (me // NY) % NX, me % NY
    return ((z + dz) % NZ) * PLANE + ((x + dx) % NX) * NY + (y + dy) % NY


def iota(shape, dim):
    return lax.broadcasted_iota(jnp.int32, shape, dim)


def column_of(row, eye):
    return jnp.sum(jnp.where(eye, row, 0), axis=1, keepdims=True)


def exact_dot(a, b):
    return jnp.dot(a, b, precision=lax.Precision.HIGHEST, preferred_element_type=jnp.float32)


def unpack_group(src, dst, src_row, dst_row):
    block = src[pl.ds(src_row, GROUP), :].astype(jnp.float32).reshape(PLANE // 2, 2, 2, 8, WIDE)
    low = iota((1, 8, WIDE), 1) < CAP
    for half in range(2):
        even, odd = block[:, 0, half], block[:, 1, half]
        first = jnp.where(low, even, jnp.roll(odd, CAP, axis=1))
        second = jnp.where(low, jnp.roll(even, CAP, axis=1), odd)
        for i, part in enumerate((first, second)):
            lane = (2 * half + i) * WIDE
            dst[pl.ds(dst_row, PLANE * CAP), lane : lane + WIDE] = part.reshape(PLANE * CAP, WIDE).astype(jnp.bfloat16)


def slot_codes(meta, base):
    table = meta[...].reshape(OWN, 128).astype(jnp.float32)
    spread = (iota((SLOTS, OWN), 0) // CAP == iota((SLOTS, OWN), 1)).astype(jnp.float32)
    wide = exact_dot(spread, table)
    pick = iota((SLOTS, 128), 1) == base + iota((SLOTS, 128), 0) % CAP
    column = jnp.sum(jnp.where(pick, wide, 0.0), axis=1, keepdims=True)
    spread_t = (iota((OWN, SLOTS), 1) // CAP == iota((OWN, SLOTS), 0)).astype(jnp.float32)
    tall = exact_dot(table.T, spread_t)
    pick_t = iota((128, SLOTS), 0) == base + iota((128, SLOTS), 1) % CAP
    row = jnp.sum(jnp.where(pick_t, tall, 0.0), axis=0, keepdims=True)
    return column, row


def kernel(
    emb, cl_ref, ord_ref, out_ref,
    x_vm, send, recv, recv2, unit_q, unit_k, meta_s, meta_r, meta_r2, res_s, res_r, key_code,
    in_sem, pay_s, pay_r, meta_ss, meta_rs, res_ss, res_rs, fwd_s, fwd_r, mfwd_s, mfwd_r,
):
    rep, me = lax.axis_index("rep"), lax.axis_index("own")
    my_z = me // PLANE
    other = 1 - rep
    base = (me % 32) * CAP

    load = pltpu.make_async_copy(emb, x_vm, in_sem)
    load.start()
    barrier = pltpu.get_barrier_semaphore()
    pl.semaphore_signal(barrier, inc=1, device_id=(other, me), device_id_type=MESH)

    def greet(k, carry):
        to = peer_of(me, k // PLANE, (k // NY) % NX, k % NY)
        pl.semaphore_signal(barrier, inc=1, device_id=(rep, to), device_id_type=MESH)
        return carry

    lax.fori_loop(1, OWN, greet, 0)

    cl_row, ord_row = cl_ref[...], ord_ref[...]
    square = (ROWS, ROWS)
    eye = iota(square, 0) == iota(square, 1)
    own_row = cl_row // CL_DEV
    own_col = column_of(own_row, eye)
    earlier = (own_col == own_row) & (iota(square, 0) < iota(square, 1))
    slot_row = jnp.sum(earlier.astype(jnp.int32), axis=0, keepdims=True)
    placed_row = own_row * CAP + slot_row
    code_row = (cl_row % CL_DEV) * 65536 + ord_row
    placed_col = column_of(placed_row, eye)
    code_col = column_of(code_row, eye)
    sent = placed_col == iota((ROWS, SLOTS), 1)
    codes = jnp.sum(jnp.where(sent, code_col + 1, 0), axis=0, keepdims=True) - 1
    for c in range(4):
        meta_s[c] = codes[:, 128 * c : 128 * c + 128]

    load.wait()
    values = x_vm[...].astype(jnp.float32)
    scale = lax.rsqrt(jnp.sum(values * values, axis=1, keepdims=True) + 1e-06)
    unit = (values * scale).astype(jnp.bfloat16)
    place = (iota((SLOTS, ROWS), 0) == placed_row).astype(jnp.bfloat16)
    low = iota((1, 8, WIDE), 1) < CAP
    evens, odds = [], []
    for half in range(2):
        first, second = (
            jnp.dot(place, unit[:, q * WIDE : (q + 1) * WIDE], preferred_element_type=jnp.float32).reshape(
                OWN // 2, 8, WIDE
            )
            for q in (2 * half, 2 * half + 1)
        )
        evens.append(jnp.where(low, first, jnp.roll(second, CAP, axis=1)))
        odds.append(jnp.where(low, jnp.roll(first, CAP, axis=1), second))
    packed = jnp.stack([jnp.stack(evens, axis=1), jnp.stack(odds, axis=1)], axis=1)
    send[...] = packed.reshape(OWN * MSG, WIDE).astype(jnp.bfloat16)

    pl.semaphore_wait(barrier, OWN)

    def send_meta(k, carry):
        to = peer_of(me, k // PLANE, (k // NY) % NX, k % NY)
        pltpu.make_async_remote_copy(
            src_ref=meta_s.at[to // 32], dst_ref=meta_r.at[me], send_sem=meta_ss, recv_sem=meta_rs,
            device_id=(rep, to), device_id_type=MESH,
        ).start()
        return carry

    lax.fori_loop(1, OWN, send_meta, 0)
    for dz in Z_ORDER:

        def send_block(k, carry, dz=dz):
            to = peer_of(me, dz, k // NY, k % NY)
            pltpu.make_async_remote_copy(
                src_ref=send.at[pl.ds(pl.multiple_of(to * MSG, MSG), MSG)],
                dst_ref=recv.at[pl.ds(pl.multiple_of(me * MSG, MSG), MSG)],
                send_sem=pay_s, recv_sem=pay_r.at[dz], device_id=(rep, to), device_id_type=MESH,
            ).start()
            return carry

        lax.fori_loop(1 if dz == 0 else 0, PLANE, send_block, 0)

    mine = pl.ds(pl.multiple_of(me * MSG, MSG), MSG)
    recv[mine, :] = send[mine, :]
    meta_r[me] = meta_s[me // 32]

    def landed(ref, n, sem):
        part = ref.at[pl.ds(0, n)]
        pltpu.make_async_copy(part, part, sem).wait()

    landed(meta_r, OWN - 1, meta_rs)
    landed(meta_r, OWN - 1, meta_ss)
    meta_fwd = pltpu.make_async_remote_copy(
        src_ref=meta_r, dst_ref=meta_r2, send_sem=mfwd_s, recv_sem=mfwd_r,
        device_id=(other, me), device_id_type=MESH,
    )
    meta_fwd.start()
    key_code[pl.ds(0, SLOTS), :], query_row = (lambda c, r: (jnp.broadcast_to(c, (SLOTS, 128)), r))(
        *slot_codes(meta_r, base)
    )
    meta_fwd.wait()
    key_code[pl.ds(SLOTS, SLOTS), :] = jnp.broadcast_to(slot_codes(meta_r2, base)[0], (SLOTS, 128))
    query_low = jnp.floor(query_row * (1.0 / 65536)) * 65536

    forwards = []
    for dz in Z_ORDER:
        z = (my_z + NZ - dz) % NZ
        start = pl.multiple_of(z * GROUP, GROUP)
        landed(recv, GROUP - (MSG if dz == 0 else 0), pay_r.at[dz])
        forward = pltpu.make_async_remote_copy(
            src_ref=recv.at[pl.ds(start, GROUP)], dst_ref=recv2.at[pl.ds(start, GROUP)],
            send_sem=fwd_s.at[dz], recv_sem=fwd_r.at[dz], device_id=(other, me), device_id_type=MESH,
        )
        forward.start()
        forwards.append((forward, z, start))
        unpack_group(recv, unit_q, start, pl.multiple_of(z * PLANE * CAP, PLANE * CAP))
    for forward, z, start in forwards:
        forward.wait()
        unpack_group(recv2, unit_k, start, pl.multiple_of(z * PLANE * CAP, PLANE * CAP))

    best = jnp.full((8, SLOTS), -1.0, jnp.float32)
    for side, keys in enumerate((unit_q, unit_k)):
        for b in range(2):
            similar = lax.dot_general(
                keys[pl.ds(256 * b, 256), :], unit_q[...], (((1,), (1,)), ((), ())),
                preferred_element_type=jnp.float32,
            )
            code = key_code[pl.ds(SLOTS * side + 256 * b, 256), 0:1]
            allowed = (code >= query_low) & (code < query_row)
            similar = jnp.where(allowed, similar, -1.0).reshape(32, 8, SLOTS)
            best = jnp.maximum(best, jnp.max(similar, axis=0))
    best = jnp.max(best, axis=0, keepdims=True)
    for c in range(4):
        res_s[c] = best[:, 128 * c : 128 * c + 128]

    def send_best(k, carry):
        to = peer_of(me, k // PLANE, (k // NY) % NX, k % NY)
        pltpu.make_async_remote_copy(
            src_ref=res_s.at[to // 32], dst_ref=res_r.at[me], send_sem=res_ss, recv_sem=res_rs,
            device_id=(rep, to), device_id_type=MESH,
        ).start()
        return carry

    lax.fori_loop(1, OWN, send_best, 0)
    res_r[me] = res_s[me // 32]
    landed(send, (OWN - 1) * MSG, pay_s)
    landed(res_r, OWN - 1, res_ss)
    landed(res_r, OWN - 1, res_rs)

    home = res_r[...].reshape(OWN, 128)
    lane = iota((OWN, 128), 1)
    owner_here = iota((OWN, ROWS), 0) == own_row
    nearest = jnp.zeros((OWN, ROWS), jnp.float32)
    for s in range(CAP):
        value = jnp.sum(jnp.where(lane == base + s, home, 0.0), axis=1, keepdims=True)
        nearest = jnp.where(owner_here & (slot_row == s), value, nearest)
    out_ref[...] = jnp.sum(nearest, axis=0, keepdims=True)


def body(embeddings, cluster, order):
    vmem = pl.BlockSpec(memory_space=pltpu.VMEM)
    dma = pltpu.SemaphoreType.DMA
    result = pl.pallas_call(
        kernel,
        out_shape=jax.ShapeDtypeStruct((1, ROWS), jnp.float32),
        in_specs=[pl.BlockSpec(memory_space=pl.ANY), vmem, vmem],
        out_specs=vmem,
        scratch_shapes=[
            pltpu.VMEM((ROWS, D), jnp.bfloat16),
            pltpu.VMEM((OWN * MSG, WIDE), jnp.bfloat16),
            pltpu.VMEM((OWN * MSG, WIDE), jnp.bfloat16),
            pltpu.VMEM((OWN * MSG, WIDE), jnp.bfloat16),
            pltpu.VMEM((SLOTS, D), jnp.bfloat16),
            pltpu.VMEM((SLOTS, D), jnp.bfloat16),
            pltpu.VMEM((4, 1, 128), jnp.int32),
            pltpu.VMEM((OWN, 1, 128), jnp.int32),
            pltpu.VMEM((OWN, 1, 128), jnp.int32),
            pltpu.VMEM((4, 1, 128), jnp.float32),
            pltpu.VMEM((OWN, 1, 128), jnp.float32),
            pltpu.VMEM((2 * SLOTS, 128), jnp.float32),
            dma, dma, dma((NZ,)), dma, dma, dma, dma, dma((NZ,)), dma((NZ,)), dma, dma,
        ],
        compiler_params=pltpu.CompilerParams(
            collective_id=0, has_side_effects=True, vmem_limit_bytes=48 * 2**20
        ),
    )(embeddings, cluster.reshape(1, ROWS), order.reshape(1, ROWS))
    return result.reshape(ROWS)


def solution(mesh):
    placed = (P(("rep", "own"), None), P(("rep", "own")), P(("rep", "own")))
    return jax.shard_map(body, mesh=mesh, in_specs=placed, out_specs=P(("rep", "own")), check_vma=False)
```

time: 138 us -> 62.1 us (0.45)
  Pallas kernels: 0 us -> 59.6 us
  blocking collectives: 54.7 us -> 0 us
  waiting for transfers between devices: 24.3 us -> 0 us
  starting transfers between devices: 20.3 us -> 0 us
  between operations: 13.6 us -> 0.01 us
  local copies, waits for them, and re-layouts: 11 us -> 2.3 us
  other arithmetic: 8.54 us -> 0 us
  matrix products: 4.67 us -> 0 us
    pallas_call x0 -> x1, Pallas kernels: none -> 59.6 us  [body(): pl.pallas_call(kernel, out_shape=jax.ShapeDtypeStruct((1, ROWS), jnp.floa...]
    all_to_all x1 -> x0, blocking collectives: 44.7 us -> none  [body(): lax.all_to_all(send_unit, 'own', split_axis=0, concat_axis=0, tiled=True)]
    all_to_all x3 -> x0, waiting for transfers between devices: 24.3 us -> none  [the longest x1 10.7 us: body(): lax.all_to_all(best_rows.reshape(owners, capacity), 'own', split_axis=0,...]
    all_to_all x3 -> x0, starting transfers between devices: 20.3 us -> none  [the longest x1 8.03 us: body(): lax.all_to_all(send_order, 'own', split_axis=0, concat_axis=0, tiled=True)]
    all_gather x2 -> x0, blocking collectives: 9.92 us -> none  [the longest x1 5.63 us: body(): lax.all_gather(query_cluster, 'rep', axis=0, tiled=True)]
    dot_general x2 -> x0, matrix products: 4.67 us -> none  [step_keys(): lax.dot_general(query_unit, block_unit, (((1,), (1,)), ((), ())), preferr...]
    all_to_all x5 -> x0, local copies, waits for them, and re-layouts: 3.2 us -> none  [the longest x2 1.24 us: body(): lax.all_to_all(send_cluster, 'own', split_axis=0, concat_axis=0, tiled=True)]
    scatter x2 -> x0, local copies, waits for them, and re-layouts: 3.1 us -> none  [the longest x1 1.55 us: body(): jnp.zeros((owners * capacity,), jnp.int32).at[placed].set(order)]
  transfers between devices with their start and end apart: 4 -> 0, of which waited for: 3 -> 0; matrix products, arithmetic and copies ran while one was open for 4% -> 0% of each run, Pallas kernels for 0% -> 0%
where the time goes in v1:
time: 62.1 us; the launch traced here: 61.9 us
  Pallas kernels  59.6 us (96%)
  local copies, waits for them, and re-layouts  2.3 us (4%)
    pallas_call x1, Pallas kernels, body(): pl.pallas_call(kernel, out_shape=jax.ShapeDtypeStruct((1, ROWS), jnp.floa...  59.6 us
    unnamed x7, local copies, waits for them, and re-layouts  2.3 us

profile of v1, /device:TPU:1, one launch (start us, length us, event | category | flops | bytes accessed | tf_op | source)
XLA Modules:
  0.0 61.9 jit_solution(11395700437365672628)
XLA Ops:
  0.0 0.0 copy-start.2
  0.0 0.0 copy-start.1
  0.0 0.7 %copy-done.2 = s32[256]{0:T(256)S(1)} copy-done((s32[256]{0:T(256)S(1)}, s32[256]{0:T(256)}, u32[]{:S(2)}) %copy-start.2) | copy-done | bytes 1048
  0.7 0.0 copy-done.1
  0.7 0.0 copy-start
  0.7 1.0 %copy-done = bf16[256,1024]{1,0:T(8,128)(2,1)S(1)} copy-done((bf16[256,1024]{1,0:T(8,128)(2,1)S(1)}, bf16[256,1024]{1,0:T(8,128)(2,1)}, u32[]{:S(2)}) %copy-start) | copy-done | bytes 524312
  1.7 59.6 %shard_map.37 = f32[1,256]{1,0:T(1,128)S(1)} custom-call(bf16[256,1024]{1,0:T(8,128)(2,1)S(1)} %copy-done, s32[1,256]{1,0:T(1,128)S(1)} %bitcast.4, s32[1,256]{1,0:T(1,128)S(1)} %bitcast.5), custom_call_target="tpu_custom_call" | custom-call | tf_op jit(solution)/shard_map/pallas_call | solution.py:226
  61.4 0.6 copy.5
Async XLA Ops:
  0.0 0.7 %copy-start.2 = (s32[256]{0:T(256)S(1)}, s32[256]{0:T(256)}, u32[]{:S(2)}) copy-start(s32[256]{0:T(256)} %param.5) | copy-start | bytes 3076
  0.0 0.7 %copy-start.1 = (s32[256]{0:T(256)S(1)}, s32[256]{0:T(256)}, u32[]{:S(2)}) copy-start(s32[256]{0:T(256)} %param.4) | copy-start | bytes 3076
  0.7 1.0 %copy-start = (bf16[256,1024]{1,0:T(8,128)(2,1)S(1)}, bf16[256,1024]{1,0:T(8,128)(2,1)}, u32[]{:S(2)}) copy-start(bf16[256,1024]{1,0:T(8,128)(2,1)} %emb.1) | copy-start | bytes 1572868

commit v2 on v1

v2 whole, which is shorter than its diff:
```python
import jax
import jax.numpy as jnp
from jax import lax
from jax.experimental import pallas as pl
from jax.experimental.pallas import tpu as pltpu
from jax.sharding import PartitionSpec as P

MESH = pl.DeviceIdType.MESH
CL_DEV = 4
CAP = 4
NZ, NX, NY = 8, 4, 4
OWN = NZ * NX * NY
PLANE = NX * NY
ROWS = 256
D = 1024
SLOTS = OWN * CAP
WIDE = D // 4
MSG = 16
GROUP = PLANE * MSG
TILE = PLANE * CAP
Z_ORDER = (4, 3, 5, 2, 6, 1, 7, 0)
PLANE_ORDER = ((2, 2), (2, 1), (1, 2), (2, 3), (3, 2), (1, 1), (3, 3), (1, 3), (3, 1), (2, 0), (0, 2), (1, 0), (0, 1), (3, 0), (0, 3), (0, 0))


def iota(shape, dim):
    return lax.broadcasted_iota(jnp.int32, shape, dim)


def column_of(row, eye):
    return jnp.sum(jnp.where(eye, row, 0), axis=1, keepdims=True)


def exact_dot(a, b):
    return jnp.dot(a, b, precision=lax.Precision.HIGHEST, preferred_element_type=jnp.float32)


def unpack_group(src, dst, src_row, dst_row):
    block = src[pl.ds(src_row, GROUP), :].astype(jnp.float32).reshape(PLANE // 2, 2, 2, 8, WIDE)
    low = iota((1, 8, WIDE), 1) < CAP
    for half in range(2):
        even, odd = block[:, 0, half], block[:, 1, half]
        first = jnp.where(low, even, jnp.roll(odd, CAP, axis=1))
        second = jnp.where(low, jnp.roll(even, CAP, axis=1), odd)
        for i, part in enumerate((first, second)):
            lane = (2 * half + i) * WIDE
            dst[pl.ds(dst_row, TILE), lane : lane + WIDE] = part.reshape(TILE, WIDE).astype(jnp.bfloat16)


def source_row(slot):
    source = slot // CAP
    return (source % NY * NX + source // NY % NX) * NZ + source // PLANE


def slot_column(table, base):
    spread = (source_row(iota((SLOTS, OWN), 0)) == iota((SLOTS, OWN), 1)).astype(jnp.float32)
    pick = iota((SLOTS, 128), 1) == base + iota((SLOTS, 128), 0) % CAP
    column = jnp.sum(jnp.where(pick, exact_dot(spread, table), 0.0), axis=1, keepdims=True)
    return jnp.broadcast_to(column, (SLOTS, 128))


def slot_row_of(table, base):
    spread = (source_row(iota((OWN, SLOTS), 1)) == iota((OWN, SLOTS), 0)).astype(jnp.float32)
    pick = iota((128, SLOTS), 0) == base + iota((128, SLOTS), 1) % CAP
    return jnp.sum(jnp.where(pick, exact_dot(table.T, spread), 0.0), axis=0, keepdims=True)


def kernel(
    emb, cl_in, ord_in, out_ref,
    x_vm, cl_ref, ord_ref, send, recv, recv2, unit_q, unit_k, code_s, code_r, code_r2, res_s, res_r, own_code, code_tmp, far_code,
    in_sem, pay_s, pay_r, code_ss, code_rs, res_ss, res_rs, fwd_s, fwd_r, cfwd_s, cfwd_r,
):
    rep, me = lax.axis_index("rep"), lax.axis_index("own")
    my_z, my_x, my_y = me // PLANE, me // NY % NX, me % NY
    other = 1 - rep
    base = (me % 32) * CAP
    z_at = [(my_z + d) % NZ for d in range(NZ)]
    x_at = [(my_x + d) % NX for d in range(NX)]
    y_at = [(my_y + d) % NY for d in range(NY)]
    z_row = [z * PLANE for z in z_at]
    in_plane = [x_at[dx] * NY + y_at[dy] for dx, dy in PLANE_ORDER]

    def peers(dz):
        return [z_row[dz] + p for p in (in_plane[:-1] if dz == 0 else in_plane)]

    def push(src, dst, send_sem, recv_sem, to, core=rep):
        copy = pltpu.make_async_remote_copy(
            src_ref=src, dst_ref=dst, send_sem=send_sem, recv_sem=recv_sem, device_id=(core, to), device_id_type=MESH
        )
        copy.start()
        return copy

    def landed(ref, n, sem):
        part = ref.at[pl.ds(0, n)]
        pltpu.make_async_copy(part, part, sem).wait()

    barrier = pltpu.get_barrier_semaphore()
    for dz in Z_ORDER:
        for to in peers(dz):
            pl.semaphore_signal(barrier, inc=1, device_id=(rep, to), device_id_type=MESH)
    pl.semaphore_signal(barrier, inc=1, device_id=(other, me), device_id_type=MESH)
    loads = [
        pltpu.make_async_copy(src, dst, in_sem.at[i])
        for i, (src, dst) in enumerate(((cl_in, cl_ref), (ord_in, ord_ref), (emb, x_vm)))
    ]
    for load in loads:
        load.start()
    for load in loads[:2]:
        load.wait()

    cl_row, ord_row = cl_ref[...], ord_ref[...]
    square = (ROWS, ROWS)
    eye = iota(square, 0) == iota(square, 1)
    own_row = cl_row // CL_DEV
    own_col = column_of(own_row, eye)
    earlier = (own_col == own_row) & (iota(square, 0) < iota(square, 1))
    slot_row = jnp.sum(earlier.astype(jnp.int32), axis=0, keepdims=True)
    placed_row = own_row * CAP + slot_row
    code_row = (cl_row % CL_DEV) * 65536 + ord_row
    placed_col = column_of(placed_row, eye)
    code_col = column_of(code_row, eye)
    sent = placed_col == iota((ROWS, SLOTS), 1)
    codes = jnp.sum(jnp.where(sent, code_col + 1, 0), axis=0, keepdims=True) - 1
    for c in range(4):
        code_s[c] = codes[:, 128 * c : 128 * c + 128]

    loads[2].wait()
    values = x_vm[...].astype(jnp.float32)
    scale = lax.rsqrt(jnp.sum(values * values, axis=1, keepdims=True) + 1e-06)
    unit = (values * scale).astype(jnp.bfloat16)
    place = (iota((SLOTS, ROWS), 0) == placed_row).astype(jnp.bfloat16)
    low = iota((1, 8, WIDE), 1) < CAP
    evens, odds = [], []
    for half in range(2):
        first, second = (
            jnp.dot(place, unit[:, q * WIDE : (q + 1) * WIDE], preferred_element_type=jnp.float32).reshape(
                OWN // 2, 8, WIDE
            )
            for q in (2 * half, 2 * half + 1)
        )
        evens.append(jnp.where(low, first, jnp.roll(second, CAP, axis=1)))
        odds.append(jnp.where(low, jnp.roll(first, CAP, axis=1), second))
    packed = jnp.stack([jnp.stack(evens, axis=1), jnp.stack(odds, axis=1)], axis=1)
    send[...] = packed.reshape(OWN * MSG, WIDE).astype(jnp.bfloat16)

    pl.semaphore_wait(barrier, OWN)

    def push_blocks(dz):
        mine = recv.at[pl.ds(pl.multiple_of(me * MSG, MSG), MSG)]
        for to in peers(dz):
            push(send.at[pl.ds(pl.multiple_of(to * MSG, MSG), MSG)], mine, pay_s, pay_r.at[dz], to)

    for dz in range(1, NZ):
        push(code_s.at[z_at[dz] // 2], code_r.at[my_y, my_x, my_z], code_ss.at[0], code_rs.at[0], me - my_z * PLANE + z_row[dz])
    push_blocks(Z_ORDER[0])
    code_r[my_y, my_x, my_z] = code_s[my_z // 2]
    landed(code_r.at[0, 0], NZ - 1, code_rs.at[0])
    for dx in range(1, NX):
        line = code_r.at[my_y, my_x]
        push(line, line, code_ss.at[1], code_rs.at[1], me + (x_at[dx] - my_x) * NY)
    for dz in Z_ORDER[1:3]:
        push_blocks(dz)
    landed(code_r.at[0], NX - 1, code_rs.at[1])
    for dy in range(1, NY):
        line = code_r.at[my_y]
        push(line, line, code_ss.at[2], code_rs.at[2], me + y_at[dy] - my_y)
    for dz in Z_ORDER[3:]:
        push_blocks(dz)

    mine = pl.ds(pl.multiple_of(me * MSG, MSG), MSG)
    recv[mine, :] = send[mine, :]
    landed(code_r, NY - 1, code_rs.at[2])
    code_forward = push(code_r, code_r2, cfwd_s, cfwd_r, me, other)
    table = code_r[...].reshape(OWN, 128).astype(jnp.float32)
    own_code[...] = slot_column(table, base)
    query_row = slot_row_of(table, base)
    query_low = jnp.floor(query_row * (1.0 / 65536)) * 65536
    code_forward.wait()
    code_tmp[...] = slot_column(code_r2[...].reshape(OWN, 128).astype(jnp.float32), base)
    landed(code_r.at[0, 0], NZ - 1, code_ss.at[0])
    landed(code_r.at[0], NX - 1, code_ss.at[1])
    landed(code_r, NY - 1, code_ss.at[2])

    forwards = []
    for i, dz in enumerate(Z_ORDER):
        z = z_at[(NZ - dz) % NZ]
        start = pl.multiple_of(z * GROUP, GROUP)
        slots = pl.ds(pl.multiple_of(z * TILE, TILE), TILE)
        far_code[pl.ds(i * TILE, TILE), :] = code_tmp[slots, :]
        landed(recv, GROUP - (MSG if dz == 0 else 0), pay_r.at[dz])
        block = pl.ds(start, GROUP)
        forwards.append((push(recv.at[block], recv2.at[block], fwd_s.at[dz], fwd_r.at[dz], me, other), start))
        unpack_group(recv, unit_q, start, pl.multiple_of(z * TILE, TILE))

    def best_of(best, keys, code, first, count):
        similar = lax.dot_general(
            keys[pl.ds(first, count), :], unit_q[...], (((1,), (1,)), ((), ())), preferred_element_type=jnp.float32
        )
        at = code[pl.ds(first, count), 0:1]
        allowed = (at >= query_low) & (at < query_row)
        similar = jnp.where(allowed, similar, -1.0).reshape(count // 8, 8, SLOTS)
        return jnp.maximum(best, jnp.max(similar, axis=0))

    best = jnp.full((8, SLOTS), -1.0, jnp.float32)
    for first in (0, 256):
        best = best_of(best, unit_q, own_code, first, 256)
    for i, (forward, start) in enumerate(forwards):
        forward.wait()
        unpack_group(recv2, unit_k, start, i * TILE)
        if i == 3:
            best = best_of(best, unit_k, far_code, 0, 256)
        if i == 6:
            best = best_of(best, unit_k, far_code, 256, 192)
    best = best_of(best, unit_k, far_code, SLOTS - TILE, TILE)
    best = jnp.max(best, axis=0, keepdims=True)
    for c in range(4):
        res_s[c] = best[:, 128 * c : 128 * c + 128]

    for dz in Z_ORDER:
        chunk = res_s.at[z_at[dz] // 2]
        for to in peers(dz):
            push(chunk, res_r.at[me], res_ss, res_rs, to)
    res_r[me] = res_s[my_z // 2]
    landed(send, (OWN - 1) * MSG, pay_s)
    landed(res_r, OWN - 1, res_ss)
    landed(res_r, OWN - 1, res_rs)

    home = res_r[...].reshape(OWN, 128)
    lane = iota((OWN, 128), 1)
    owner_here = iota((OWN, ROWS), 0) == own_row
    nearest = jnp.zeros((OWN, ROWS), jnp.float32)
    for s in range(CAP):
        value = jnp.sum(jnp.where(lane == base + s, home, 0.0), axis=1, keepdims=True)
        nearest = jnp.where(owner_here & (slot_row == s), value, nearest)
    out_ref[...] = jnp.sum(nearest, axis=0, keepdims=True)


def body(embeddings, cluster, order):
    hbm = pl.BlockSpec(memory_space=pl.ANY)
    dma = pltpu.SemaphoreType.DMA
    blocks = pltpu.VMEM((OWN * MSG, WIDE), jnp.bfloat16)
    units = pltpu.VMEM((SLOTS, D), jnp.bfloat16)
    line = pltpu.VMEM((1, ROWS), jnp.int32)
    table = pltpu.VMEM((NY, NX, NZ, 1, 128), jnp.int32)
    codes = pltpu.VMEM((SLOTS, 128), jnp.float32)
    result = pl.pallas_call(
        kernel,
        out_shape=jax.ShapeDtypeStruct((1, ROWS), jnp.float32),
        in_specs=[hbm, hbm, hbm],
        out_specs=pl.BlockSpec(memory_space=pltpu.VMEM),
        scratch_shapes=[
            pltpu.VMEM((ROWS, D), jnp.bfloat16), line, line, blocks, blocks, blocks, units, units,
            pltpu.VMEM((4, 1, 128), jnp.int32), table, table,
            pltpu.VMEM((4, 1, 128), jnp.float32), pltpu.VMEM((OWN, 1, 128), jnp.float32), codes, codes, codes,
            dma((3,)), dma, dma((NZ,)), dma((3,)), dma((3,)), dma, dma, dma((NZ,)), dma((NZ,)), dma, dma,
        ],
        compiler_params=pltpu.CompilerParams(
            collective_id=0, has_side_effects=True, vmem_limit_bytes=60 * 2**20
        ),
    )(embeddings, cluster.reshape(1, ROWS), order.reshape(1, ROWS))
    return result.reshape(ROWS)


def solution(mesh):
    placed = (P(("rep", "own"), None), P(("rep", "own")), P(("rep", "own")))
    return jax.shard_map(body, mesh=mesh, in_specs=placed, out_specs=P(("rep", "own")), check_vma=False)
```

time: 62.1 us -> 49.9 us (0.80)
  Pallas kernels: 59.6 us -> 48.5 us
  local copies, waits for them, and re-layouts: 2.3 us -> 1.22 us
    pallas_call x1, Pallas kernels: 59.6 us -> 48.5 us  [body(): pl.pallas_call(kernel, out_shape=jax.ShapeDtypeStruct((1, ROWS), jnp.floa...]
    unnamed x7 -> x3, local copies, waits for them, and re-layouts: 2.3 us -> 1.22 us
where the time goes in v2:
time: 49.9 us; the launch traced here: 49.7 us
  Pallas kernels  48.5 us (97%)
  local copies, waits for them, and re-layouts  1.22 us (2%)
    pallas_call x1, Pallas kernels, body(): pl.pallas_call(kernel, out_shape=jax.ShapeDtypeStruct((1, ROWS), jnp.floa...  48.5 us
    unnamed x3, local copies, waits for them, and re-layouts  1.22 us

profile of v2, /device:TPU:1, one launch (start us, length us, event | category | flops | bytes accessed | tf_op | source)
XLA Modules:
  0.0 49.7 jit_solution(3686006650350602084)
XLA Ops:
  0.0 48.5 %shard_map.37 = f32[1,256]{1,0:T(1,128)} custom-call(bf16[256,1024]{1,0:T(8,128)(2,1)} %emb.1, s32[1,256]{1,0:T(1,128)} %bitcast.4, s32[1,256]{1,0:T(1,128)} %bitcast.5), custom_call_target="tpu_custom_call" | custom-call | tf_op jit(solution)/shard_map/pallas_call | solution.py:245
  48.5 0.0 copy-start
  48.5 0.7 %copy-done = f32[1,256]{1,0:T(1,128)S(1)} copy-done((f32[1,256]{1,0:T(1,128)S(1)}, f32[1,256]{1,0:T(1,128)}, u32[]{:S(2)}) %copy-start) | copy-done | bytes 1048
  49.2 0.6 %copy.5 = f32[256]{0:T(256)} copy(f32[256]{0:T(256)S(1)} %bitcast.3) | data formatting | bytes 2048
Async XLA Ops:
  48.5 0.7 %copy-start = (f32[1,256]{1,0:T(1,128)S(1)}, f32[1,256]{1,0:T(1,128)}, u32[]{:S(2)}) copy-start(f32[1,256]{1,0:T(1,128)} %shard_map.37) | copy-start | bytes 3076

commit v3 on v2

--- a/solution.py
+++ b/solution.py
@@ -19,6 +19,8 @@
 GROUP = PLANE * MSG
 TILE = PLANE * CAP
 Z_ORDER = (4, 3, 5, 2, 6, 1, 7, 0)
+LAND_ORDER = (0, 3, 5, 4, 2, 6, 1, 7)
+RELAY = 4
 PLANE_ORDER = ((2, 2), (2, 1), (1, 2), (2, 3), (3, 2), (1, 1), (3, 3), (1, 3), (3, 1), (2, 0), (0, 2), (1, 0), (0, 1), (3, 0), (0, 3), (0, 0))
 
 
@@ -66,8 +68,8 @@
 
 def kernel(
     emb, cl_in, ord_in, out_ref,
-    x_vm, cl_ref, ord_ref, send, recv, recv2, unit_q, unit_k, code_s, code_r, code_r2, res_s, res_r, own_code, code_tmp, far_code,
-    in_sem, pay_s, pay_r, code_ss, code_rs, res_ss, res_rs, fwd_s, fwd_r, cfwd_s, cfwd_r,
+    x_vm, cl_ref, ord_ref, send, recv, recv2, relay, unit_q, unit_k, code_s, code_r, code_r2, res_s, res_r, own_code, code_tmp, far_code,
+    in_sem, pay_s, pay_r, code_ss, code_rs, res_ss, res_rs, fwd_s, fwd_r, cfwd_s, cfwd_r, relay_s, relay_r, ready,
 ):
     rep, me = lax.axis_index("rep"), lax.axis_index("own")
     my_z, my_x, my_y = me // PLANE, me // NY % NX, me % NY
@@ -94,9 +96,11 @@
         pltpu.make_async_copy(part, part, sem).wait()
 
     barrier = pltpu.get_barrier_semaphore()
-    for dz in Z_ORDER:
-        for to in peers(dz):
-            pl.semaphore_signal(barrier, inc=1, device_id=(rep, to), device_id_type=MESH)
+    column = me - my_z * PLANE
+    line = [column + z_row[dz] for dz in range(NZ)]
+    near = [line[dz] for dz in Z_ORDER[:-1]] + peers(0)
+    for to in near:
+        pl.semaphore_signal(barrier, inc=1, device_id=(rep, to), device_id_type=MESH)
     pl.semaphore_signal(barrier, inc=1, device_id=(other, me), device_id_type=MESH)
     loads = [
         pltpu.make_async_copy(src, dst, in_sem.at[i])
@@ -142,30 +146,43 @@
     packed = jnp.stack([jnp.stack(evens, axis=1), jnp.stack(odds, axis=1)], axis=1)
     send[...] = packed.reshape(OWN * MSG, WIDE).astype(jnp.bfloat16)
 
-    pl.semaphore_wait(barrier, OWN)
-
-    def push_blocks(dz):
-        mine = recv.at[pl.ds(pl.multiple_of(me * MSG, MSG), MSG)]
-        for to in peers(dz):
-            push(send.at[pl.ds(pl.multiple_of(to * MSG, MSG), MSG)], mine, pay_s, pay_r.at[dz], to)
-
-    for dz in range(1, NZ):
-        push(code_s.at[z_at[dz] // 2], code_r.at[my_y, my_x, my_z], code_ss.at[0], code_rs.at[0], me - my_z * PLANE + z_row[dz])
-    push_blocks(Z_ORDER[0])
+    def block_of(ref, index):
+        return ref.at[pl.ds(pl.multiple_of(index * MSG, MSG), MSG)]
+
+    def push_blocks(*groups):
+        for pair in zip(*(peers(dz) for dz in groups)):
+            for dz, to in zip(groups, pair):
+                push(block_of(send, to), block_of(recv, me), pay_s, pay_r.at[dz], to)
+
+    pl.semaphore_wait(barrier, len(near) + 1)
+    for to in peers(0):
+        pl.semaphore_signal(ready, inc=1, device_id=(rep, to), device_id_type=MESH)
+
+    for dz in Z_ORDER[:-1]:
+        push(code_s.at[z_at[dz] // 2], code_r.at[my_y, my_x, my_z], code_ss.at[0], code_rs.at[0], line[dz])
+    opposite = send.at[pl.ds(pl.multiple_of(z_at[RELAY] * GROUP, GROUP), GROUP)]
+    relayed = push(opposite, relay, relay_s, relay_r, line[RELAY])
+    push_blocks(0)
+    pl.semaphore_wait(ready, PLANE - 1)
+    push_blocks(3, 5)
     code_r[my_y, my_x, my_z] = code_s[my_z // 2]
     landed(code_r.at[0, 0], NZ - 1, code_rs.at[0])
     for dx in range(1, NX):
-        line = code_r.at[my_y, my_x]
-        push(line, line, code_ss.at[1], code_rs.at[1], me + (x_at[dx] - my_x) * NY)
-    for dz in Z_ORDER[1:3]:
-        push_blocks(dz)
+        part = code_r.at[my_y, my_x]
+        push(part, part, code_ss.at[1], code_rs.at[1], me + (x_at[dx] - my_x) * NY)
+    relayed.wait()
+    source = line[RELAY]
+    for p, to in zip(in_plane, peers(0)):
+        push(block_of(relay, p), block_of(recv, source), pay_s, pay_r.at[RELAY], to)
+    push_blocks(2, 6)
     landed(code_r.at[0], NX - 1, code_rs.at[1])
     for dy in range(1, NY):
-        line = code_r.at[my_y]
-        push(line, line, code_ss.at[2], code_rs.at[2], me + y_at[dy] - my_y)
-    for dz in Z_ORDER[3:]:
-        push_blocks(dz)
-
+        part = code_r.at[my_y]
+        push(part, part, code_ss.at[2], code_rs.at[2], me + y_at[dy] - my_y)
+    push_blocks(1, 7)
+
+    handed = pl.ds(pl.multiple_of(source * MSG, MSG), MSG)
+    recv[handed, :] = relay[pl.ds(pl.multiple_of(in_plane[-1] * MSG, MSG), MSG), :]
     mine = pl.ds(pl.multiple_of(me * MSG, MSG), MSG)
     recv[mine, :] = send[mine, :]
     landed(code_r, NY - 1, code_rs.at[2])
@@ -181,12 +198,12 @@
     landed(code_r, NY - 1, code_ss.at[2])
 
     forwards = []
-    for i, dz in enumerate(Z_ORDER):
+    for i, dz in enumerate(LAND_ORDER):
         z = z_at[(NZ - dz) % NZ]
         start = pl.multiple_of(z * GROUP, GROUP)
         slots = pl.ds(pl.multiple_of(z * TILE, TILE), TILE)
         far_code[pl.ds(i * TILE, TILE), :] = code_tmp[slots, :]
-        landed(recv, GROUP - (MSG if dz == 0 else 0), pay_r.at[dz])
+        landed(recv, GROUP - (MSG if dz in (0, RELAY) else 0), pay_r.at[dz])
         block = pl.ds(start, GROUP)
         forwards.append((push(recv.at[block], recv2.at[block], fwd_s.at[dz], fwd_r.at[dz], me, other), start))
         unpack_group(recv, unit_q, start, pl.multiple_of(z * TILE, TILE))
@@ -220,7 +237,7 @@
         for to in peers(dz):
             push(chunk, res_r.at[me], res_ss, res_rs, to)
     res_r[me] = res_s[my_z // 2]
-    landed(send, (OWN - 1) * MSG, pay_s)
+    landed(send, (OWN - 2) * MSG, pay_s)
     landed(res_r, OWN - 1, res_ss)
     landed(res_r, OWN - 1, res_rs)
 
@@ -248,16 +265,18 @@
         in_specs=[hbm, hbm, hbm],
         out_specs=pl.BlockSpec(memory_space=pltpu.VMEM),
         scratch_shapes=[
-            pltpu.VMEM((ROWS, D), jnp.bfloat16), line, line, blocks, blocks, blocks, units, units,
+            pltpu.VMEM((ROWS, D), jnp.bfloat16), line, line, blocks, blocks, blocks,
+            pltpu.VMEM((GROUP, WIDE), jnp.bfloat16), units, units,
             pltpu.VMEM((4, 1, 128), jnp.int32), table, table,
             pltpu.VMEM((4, 1, 128), jnp.float32), pltpu.VMEM((OWN, 1, 128), jnp.float32), codes, codes, codes,
-            dma((3,)), dma, dma((NZ,)), dma((3,)), dma((3,)), dma, dma, dma((NZ,)), dma((NZ,)), dma, dma,
+            dma((3,)), dma, dma((NZ,)), dma((3,)), dma((3,)), dma, dma, dma((NZ,)), dma((NZ,)), dma, dma, dma, dma,
+            pltpu.SemaphoreType.REGULAR,
         ],
         compiler_params=pltpu.CompilerParams(
             collective_id=0, has_side_effects=True, vmem_limit_bytes=60 * 2**20
         ),
     )(embeddings, cluster.reshape(1, ROWS), order.reshape(1, ROWS))
-    return result.reshape(ROWS)
+    return jnp.maximum(result.reshape(ROWS), -1.0)
 
 
 def solution(mesh):

time: 49.9 us -> 47.9 us (0.960)
  Pallas kernels: 48.5 us -> 46.5 us
  other arithmetic: 0 us -> 1.24 us
  local copies, waits for them, and re-layouts: 1.22 us -> 0 us
    pallas_call x1, Pallas kernels: 48.5 us -> 46.5 us  [body(): pl.pallas_call(kernel, out_shape=jax.ShapeDtypeStruct((1, ROWS), jnp.floa...]
    max x0 -> x1, other arithmetic: none -> 1.24 us  [body(): return jnp.maximum(result.reshape(ROWS), -1.0)]
    unnamed x3 -> x0, local copies, waits for them, and re-layouts: 1.22 us -> none
where the time goes in v3:
time: 47.9 us; the launch traced here: 47.8 us
  Pallas kernels  46.5 us (97%)
  other arithmetic  1.24 us (3%)
    pallas_call x1, Pallas kernels, body(): pl.pallas_call(kernel, out_shape=jax.ShapeDtypeStruct((1, ROWS), jnp.floa...  46.5 us
    max x1, other arithmetic, body(): return jnp.maximum(result.reshape(ROWS), -1.0)  1.24 us

profile of v3, /device:TPU:1, one launch (start us, length us, event | category | flops | bytes accessed | tf_op | source)
XLA Modules:
  0.0 47.8 jit_solution(1385067755333256643)
XLA Ops:
  0.0 46.5 %shard_map.37 = f32[1,256]{1,0:T(1,128)} custom-call(bf16[256,1024]{1,0:T(8,128)(2,1)} %emb.1, s32[1,256]{1,0:T(1,128)} %bitcast.3, s32[1,256]{1,0:T(1,128)} %bitcast.4), custom_call_target="tpu_custom_call" | custom-call | tf_op jit(solution)/shard_map/pallas_call | solution.py:262
  46.5 1.2 %broadcast_maximum_fusion = f32[1,256]{1,0:T(1,128)} fusion(f32[1,256]{1,0:T(1,128)} %shard_map.37), kind=kLoop, calls=%fused_computation | loop fusion | flops 256 | bytes 2048 | tf_op jit(solution)/shard_map/max | solution.py:279

commit v4 on v3

--- a/solution.py
+++ b/solution.py
@@ -19,8 +19,9 @@
 GROUP = PLANE * MSG
 TILE = PLANE * CAP
 Z_ORDER = (4, 3, 5, 2, 6, 1, 7, 0)
-LAND_ORDER = (0, 3, 5, 4, 2, 6, 1, 7)
-RELAY = 4
+LAND_ORDER = (0, 1, 7, 3, 5, 4, 2, 6)
+RELAYS = (1, 7, 4)
+VMEM_BYTES = 55226 * 2**10
 PLANE_ORDER = ((2, 2), (2, 1), (1, 2), (2, 3), (3, 2), (1, 1), (3, 3), (1, 3), (3, 1), (2, 0), (0, 2), (1, 0), (0, 1), (3, 0), (0, 3), (0, 0))
 
 
@@ -160,8 +161,22 @@
 
     for dz in Z_ORDER[:-1]:
         push(code_s.at[z_at[dz] // 2], code_r.at[my_y, my_x, my_z], code_ss.at[0], code_rs.at[0], line[dz])
-    opposite = send.at[pl.ds(pl.multiple_of(z_at[RELAY] * GROUP, GROUP), GROUP)]
-    relayed = push(opposite, relay, relay_s, relay_r, line[RELAY])
+    blocks = [
+        push(
+            send.at[pl.ds(pl.multiple_of(z_at[dz] * GROUP, GROUP), GROUP)], relay.at[pl.ds(i * GROUP, GROUP)],
+            relay_s.at[i], relay_r.at[i], line[dz],
+        )
+        for i, dz in enumerate(RELAYS)
+    ]
+
+    def hand_on(i):
+        blocks[i].wait()
+        source = line[(NZ - RELAYS[i]) % NZ]
+        for p, to in zip(in_plane, peers(0)):
+            push(block_of(relay, i * PLANE + p), block_of(recv, source), pay_s, pay_r.at[RELAYS[i]], to)
+        kept = pl.ds(pl.multiple_of(i * GROUP + in_plane[-1] * MSG, MSG), MSG)
+        recv[pl.ds(pl.multiple_of(source * MSG, MSG), MSG), :] = relay[kept, :]
+
     push_blocks(0)
     pl.semaphore_wait(ready, PLANE - 1)
     push_blocks(3, 5)
@@ -170,19 +185,15 @@
     for dx in range(1, NX):
         part = code_r.at[my_y, my_x]
         push(part, part, code_ss.at[1], code_rs.at[1], me + (x_at[dx] - my_x) * NY)
-    relayed.wait()
-    source = line[RELAY]
-    for p, to in zip(in_plane, peers(0)):
-        push(block_of(relay, p), block_of(recv, source), pay_s, pay_r.at[RELAY], to)
-    push_blocks(2, 6)
+    hand_on(0)
+    hand_on(1)
     landed(code_r.at[0], NX - 1, code_rs.at[1])
     for dy in range(1, NY):
         part = code_r.at[my_y]
         push(part, part, code_ss.at[2], code_rs.at[2], me + y_at[dy] - my_y)
-    push_blocks(1, 7)
-
-    handed = pl.ds(pl.multiple_of(source * MSG, MSG), MSG)
-    recv[handed, :] = relay[pl.ds(pl.multiple_of(in_plane[-1] * MSG, MSG), MSG), :]
+    hand_on(2)
+    push_blocks(2, 6)
+
     mine = pl.ds(pl.multiple_of(me * MSG, MSG), MSG)
     recv[mine, :] = send[mine, :]
     landed(code_r, NY - 1, code_rs.at[2])
@@ -203,7 +214,7 @@
         start = pl.multiple_of(z * GROUP, GROUP)
         slots = pl.ds(pl.multiple_of(z * TILE, TILE), TILE)
         far_code[pl.ds(i * TILE, TILE), :] = code_tmp[slots, :]
-        landed(recv, GROUP - (MSG if dz in (0, RELAY) else 0), pay_r.at[dz])
+        landed(recv, GROUP - (MSG if dz in (0, *RELAYS) else 0), pay_r.at[dz])
         block = pl.ds(start, GROUP)
         forwards.append((push(recv.at[block], recv2.at[block], fwd_s.at[dz], fwd_r.at[dz], me, other), start))
         unpack_group(recv, unit_q, start, pl.multiple_of(z * TILE, TILE))
@@ -237,7 +248,7 @@
         for to in peers(dz):
             push(chunk, res_r.at[me], res_ss, res_rs, to)
     res_r[me] = res_s[my_z // 2]
-    landed(send, (OWN - 2) * MSG, pay_s)
+    landed(send, (OWN - 1 - len(RELAYS)) * MSG, pay_s)
     landed(res_r, OWN - 1, res_ss)
     landed(res_r, OWN - 1, res_rs)
 
@@ -266,17 +277,18 @@
         out_specs=pl.BlockSpec(memory_space=pltpu.VMEM),
         scratch_shapes=[
             pltpu.VMEM((ROWS, D), jnp.bfloat16), line, line, blocks, blocks, blocks,
-            pltpu.VMEM((GROUP, WIDE), jnp.bfloat16), units, units,
+            pltpu.VMEM((len(RELAYS) * GROUP, WIDE), jnp.bfloat16), units, units,
             pltpu.VMEM((4, 1, 128), jnp.int32), table, table,
             pltpu.VMEM((4, 1, 128), jnp.float32), pltpu.VMEM((OWN, 1, 128), jnp.float32), codes, codes, codes,
-            dma((3,)), dma, dma((NZ,)), dma((3,)), dma((3,)), dma, dma, dma((NZ,)), dma((NZ,)), dma, dma, dma, dma,
+            dma((3,)), dma, dma((NZ,)), dma((3,)), dma((3,)), dma, dma, dma((NZ,)), dma((NZ,)), dma, dma,
+            dma((len(RELAYS),)), dma((len(RELAYS),)),
             pltpu.SemaphoreType.REGULAR,
         ],
         compiler_params=pltpu.CompilerParams(
-            collective_id=0, has_side_effects=True, vmem_limit_bytes=60 * 2**20
+            collective_id=0, has_side_effects=True, vmem_limit_bytes=VMEM_BYTES
         ),
     )(embeddings, cluster.reshape(1, ROWS), order.reshape(1, ROWS))
-    return jnp.maximum(result.reshape(ROWS), -1.0)
+    return result.reshape(ROWS)
 
 
 def solution(mesh):

time: 47.9 us -> 45.8 us (0.956)
  Pallas kernels: 46.5 us -> 45.1 us
  other arithmetic: 1.24 us -> 0 us
  local copies, waits for them, and re-layouts: 0 us -> 0.56 us
    pallas_call x1, Pallas kernels: 46.5 us -> 45.1 us  [body(): pl.pallas_call(kernel, out_shape=jax.ShapeDtypeStruct((1, ROWS), jnp.floa...]
    max x1 -> x0, other arithmetic: 1.24 us -> none  [body(): return jnp.maximum(result.reshape(ROWS), -1.0)]
    unnamed x0 -> x1, local copies, waits for them, and re-layouts: none -> 0.56 us
where the time goes in v4:
time: 45.8 us; the launch traced here: 45.7 us
  Pallas kernels  45.1 us (98%)
  local copies, waits for them, and re-layouts  0.56 us (1%)
    pallas_call x1, Pallas kernels, body(): pl.pallas_call(kernel, out_shape=jax.ShapeDtypeStruct((1, ROWS), jnp.floa...  45.1 us

profile of v4, /device:TPU:1, one launch (start us, length us, event | category | flops | bytes accessed | tf_op | source)
XLA Modules:
  0.0 45.7 jit_solution(808339797176467330)
XLA Ops:
  0.0 45.1 %shard_map.37 = f32[1,256]{1,0:T(1,128)S(1)} custom-call(bf16[256,1024]{1,0:T(8,128)(2,1)} %emb.1, s32[1,256]{1,0:T(1,128)} %bitcast.4, s32[1,256]{1,0:T(1,128)} %bitcast.5), custom_call_target="tpu_custom_call" | custom-call | tf_op jit(solution)/shard_map/pallas_call | solution.py:273
  45.2 0.6 %copy.5 = f32[256]{0:T(256)} copy(f32[256]{0:T(256)S(1)} %bitcast.3) | data formatting | bytes 2048

commit v5 on v4

--- a/solution.py
+++ b/solution.py
@@ -19,8 +19,8 @@
 GROUP = PLANE * MSG
 TILE = PLANE * CAP
 Z_ORDER = (4, 3, 5, 2, 6, 1, 7, 0)
-LAND_ORDER = (0, 1, 7, 3, 5, 4, 2, 6)
-RELAYS = (1, 7, 4)
+LAND_ORDER = (0, 2, 6, 3, 5, 4, 1, 7)
+RELAYS = (2, 6)
 VMEM_BYTES = 55226 * 2**10
 PLANE_ORDER = ((2, 2), (2, 1), (1, 2), (2, 3), (3, 2), (1, 1), (3, 3), (1, 3), (3, 1), (2, 0), (0, 2), (1, 0), (0, 1), (3, 0), (0, 3), (0, 0))
 
@@ -99,7 +99,9 @@
     barrier = pltpu.get_barrier_semaphore()
     column = me - my_z * PLANE
     line = [column + z_row[dz] for dz in range(NZ)]
-    near = [line[dz] for dz in Z_ORDER[:-1]] + peers(0)
+    x_line = [me + (x_at[d] - my_x) * NY for d in range(1, NX)]
+    y_line = [me + y_at[d] - my_y for d in range(1, NY)]
+    near = [line[dz] for dz in (2, 6, 1, 7)] + x_line + y_line
     for to in near:
         pl.semaphore_signal(barrier, inc=1, device_id=(rep, to), device_id_type=MESH)
     pl.semaphore_signal(barrier, inc=1, device_id=(other, me), device_id_type=MESH)
@@ -156,11 +158,9 @@
                 push(block_of(send, to), block_of(recv, me), pay_s, pay_r.at[dz], to)
 
     pl.semaphore_wait(barrier, len(near) + 1)
-    for to in peers(0):
-        pl.semaphore_signal(ready, inc=1, device_id=(rep, to), device_id_type=MESH)
-
-    for dz in Z_ORDER[:-1]:
-        push(code_s.at[z_at[dz] // 2], code_r.at[my_y, my_x, my_z], code_ss.at[0], code_rs.at[0], line[dz])
+    for to in (line[2], line[6]):
+        pl.semaphore_signal(ready.at[0], inc=1, device_id=(rep, to), device_id_type=MESH)
+
     blocks = [
         push(
             send.at[pl.ds(pl.multiple_of(z_at[dz] * GROUP, GROUP), GROUP)], relay.at[pl.ds(i * GROUP, GROUP)],
@@ -169,6 +169,12 @@
         for i, dz in enumerate(RELAYS)
     ]
 
+    pl.semaphore_wait(ready.at[0], 2)
+    for to in x_line:
+        pl.semaphore_signal(ready.at[1], inc=1, device_id=(rep, to), device_id_type=MESH)
+    for dz in Z_ORDER[:-1]:
+        push(code_s.at[z_at[dz] // 2], code_r.at[my_y, my_x, my_z], code_ss.at[0], code_rs.at[0], line[dz])
+
     def hand_on(i):
         blocks[i].wait()
         source = line[(NZ - RELAYS[i]) % NZ]
@@ -177,8 +183,11 @@
         kept = pl.ds(pl.multiple_of(i * GROUP + in_plane[-1] * MSG, MSG), MSG)
         recv[pl.ds(pl.multiple_of(source * MSG, MSG), MSG), :] = relay[kept, :]
 
+    pl.semaphore_wait(ready.at[1], NX - 1)
+    for to in y_line:
+        pl.semaphore_signal(ready.at[2], inc=1, device_id=(rep, to), device_id_type=MESH)
+    pl.semaphore_wait(ready.at[2], NY - 1)
     push_blocks(0)
-    pl.semaphore_wait(ready, PLANE - 1)
     push_blocks(3, 5)
     code_r[my_y, my_x, my_z] = code_s[my_z // 2]
     landed(code_r.at[0, 0], NZ - 1, code_rs.at[0])
@@ -187,12 +196,12 @@
         push(part, part, code_ss.at[1], code_rs.at[1], me + (x_at[dx] - my_x) * NY)
     hand_on(0)
     hand_on(1)
+    push_blocks(4)
     landed(code_r.at[0], NX - 1, code_rs.at[1])
     for dy in range(1, NY):
         part = code_r.at[my_y]
         push(part, part, code_ss.at[2], code_rs.at[2], me + y_at[dy] - my_y)
-    hand_on(2)
-    push_blocks(2, 6)
+    push_blocks(1, 7)
 
     mine = pl.ds(pl.multiple_of(me * MSG, MSG), MSG)
     recv[mine, :] = send[mine, :]
@@ -282,7 +291,7 @@
             pltpu.VMEM((4, 1, 128), jnp.float32), pltpu.VMEM((OWN, 1, 128), jnp.float32), codes, codes, codes,
             dma((3,)), dma, dma((NZ,)), dma((3,)), dma((3,)), dma, dma, dma((NZ,)), dma((NZ,)), dma, dma,
             dma((len(RELAYS),)), dma((len(RELAYS),)),
-            pltpu.SemaphoreType.REGULAR,
+            pltpu.SemaphoreType.REGULAR((3,)),
         ],
         compiler_params=pltpu.CompilerParams(
             collective_id=0, has_side_effects=True, vmem_limit_bytes=VMEM_BYTES

time: 45.8 us -> 44.8 us (0.978)
  Pallas kernels: 45.1 us -> 44.1 us
    pallas_call x1, Pallas kernels: 45.1 us -> 44.1 us  [body(): pl.pallas_call(kernel, out_shape=jax.ShapeDtypeStruct((1, ROWS), jnp.floa...]
where the time goes in v5:
time: 44.8 us; the launch traced here: 44.7 us
  Pallas kernels  44.1 us (98%)
  local copies, waits for them, and re-layouts  0.56 us (1%)
    pallas_call x1, Pallas kernels, body(): pl.pallas_call(kernel, out_shape=jax.ShapeDtypeStruct((1, ROWS), jnp.floa...  44.1 us

profile of v5, /device:TPU:1, one launch (start us, length us, event | category | flops | bytes accessed | tf_op | source)
XLA Modules:
  0.0 44.7 jit_solution(7525408675761749335)
XLA Ops:
  0.0 44.1 %shard_map.37 = f32[1,256]{1,0:T(1,128)S(1)} custom-call(bf16[256,1024]{1,0:T(8,128)(2,1)} %emb.1, s32[1,256]{1,0:T(1,128)} %bitcast.4, s32[1,256]{1,0:T(1,128)} %bitcast.5), custom_call_target="tpu_custom_call" | custom-call | tf_op jit(solution)/shard_map/pallas_call | solution.py:282
  44.1 0.6 %copy.5 = f32[256]{0:T(256)} copy(f32[256]{0:T(256)S(1)} %bitcast.3) | data formatting | bytes 2048

commit v6 on v5

--- a/solution.py
+++ b/solution.py
@@ -49,6 +49,10 @@
             dst[pl.ds(dst_row, TILE), lane : lane + WIDE] = part.reshape(TILE, WIDE).astype(jnp.bfloat16)
 
 
+def choose(index, values):
+    return sum(jnp.where(index == i, value, 0) for i, value in enumerate(values))
+
+
 def source_row(slot):
     source = slot // CAP
     return (source % NY * NX + source // NY % NX) * NZ + source // PLANE
@@ -122,6 +126,54 @@
     earlier = (own_col == own_row) & (iota(square, 0) < iota(square, 1))
     slot_row = jnp.sum(earlier.astype(jnp.int32), axis=0, keepdims=True)
     placed_row = own_row * CAP + slot_row
+    loads[2].wait()
+    values = x_vm[...].astype(jnp.float32)
+    scale = lax.rsqrt(jnp.sum(values * values, axis=1, keepdims=True) + 1e-06)
+    unit = (values * scale).astype(jnp.bfloat16)
+    low = iota((1, 8, WIDE), 1) < CAP
+
+    def pack(*groups):
+        count = len(groups) * TILE
+        index = iota((count, ROWS), 0)
+        slot = choose(index // TILE, [z_at[dz] * TILE for dz in groups]) + index % TILE
+        place = (slot == placed_row).astype(jnp.bfloat16)
+        evens, odds = [], []
+        for half in range(2):
+            first, second = (
+                jnp.dot(place, unit[:, q * WIDE : (q + 1) * WIDE], preferred_element_type=jnp.float32).reshape(
+                    count // 8, 8, WIDE
+                )
+                for q in (2 * half, 2 * half + 1)
+            )
+            evens.append(jnp.where(low, first, jnp.roll(second, CAP, axis=1)))
+            odds.append(jnp.where(low, jnp.roll(first, CAP, axis=1), second))
+        packed = jnp.stack([jnp.stack(evens, axis=1), jnp.stack(odds, axis=1)], axis=1)
+        packed = packed.reshape(len(groups), GROUP, WIDE).astype(jnp.bfloat16)
+        for i, dz in enumerate(groups):
+            send[pl.ds(pl.multiple_of(z_at[dz] * GROUP, GROUP), GROUP), :] = packed[i]
+
+    pack(*RELAYS)
+
+    def block_of(ref, index):
+        return ref.at[pl.ds(pl.multiple_of(index * MSG, MSG), MSG)]
+
+    def push_blocks(*groups):
+        for pair in zip(*(peers(dz) for dz in groups)):
+            for dz, to in zip(groups, pair):
+                push(block_of(send, to), block_of(recv, me), pay_s, pay_r.at[dz], to)
+
+    pl.semaphore_wait(barrier, len(near) + 1)
+    for to in (line[2], line[6]):
+        pl.semaphore_signal(ready.at[0], inc=1, device_id=(rep, to), device_id_type=MESH)
+
+    blocks = [
+        push(
+            send.at[pl.ds(pl.multiple_of(z_at[dz] * GROUP, GROUP), GROUP)], relay.at[pl.ds(i * GROUP, GROUP)],
+            relay_s.at[i], relay_r.at[i], line[dz],
+        )
+        for i, dz in enumerate(RELAYS)
+    ]
+
     code_row = (cl_row % CL_DEV) * 65536 + ord_row
     placed_col = column_of(placed_row, eye)
     code_col = column_of(code_row, eye)
@@ -129,51 +181,13 @@
     codes = jnp.sum(jnp.where(sent, code_col + 1, 0), axis=0, keepdims=True) - 1
     for c in range(4):
         code_s[c] = codes[:, 128 * c : 128 * c + 128]
-
-    loads[2].wait()
-    values = x_vm[...].astype(jnp.float32)
-    scale = lax.rsqrt(jnp.sum(values * values, axis=1, keepdims=True) + 1e-06)
-    unit = (values * scale).astype(jnp.bfloat16)
-    place = (iota((SLOTS, ROWS), 0) == placed_row).astype(jnp.bfloat16)
-    low = iota((1, 8, WIDE), 1) < CAP
-    evens, odds = [], []
-    for half in range(2):
-        first, second = (
-            jnp.dot(place, unit[:, q * WIDE : (q + 1) * WIDE], preferred_element_type=jnp.float32).reshape(
-                OWN // 2, 8, WIDE
-            )
-            for q in (2 * half, 2 * half + 1)
-        )
-        evens.append(jnp.where(low, first, jnp.roll(second, CAP, axis=1)))
-        odds.append(jnp.where(low, jnp.roll(first, CAP, axis=1), second))
-    packed = jnp.stack([jnp.stack(evens, axis=1), jnp.stack(odds, axis=1)], axis=1)
-    send[...] = packed.reshape(OWN * MSG, WIDE).astype(jnp.bfloat16)
-
-    def block_of(ref, index):
-        return ref.at[pl.ds(pl.multiple_of(index * MSG, MSG), MSG)]
-
-    def push_blocks(*groups):
-        for pair in zip(*(peers(dz) for dz in groups)):
-            for dz, to in zip(groups, pair):
-                push(block_of(send, to), block_of(recv, me), pay_s, pay_r.at[dz], to)
-
-    pl.semaphore_wait(barrier, len(near) + 1)
-    for to in (line[2], line[6]):
-        pl.semaphore_signal(ready.at[0], inc=1, device_id=(rep, to), device_id_type=MESH)
-
-    blocks = [
-        push(
-            send.at[pl.ds(pl.multiple_of(z_at[dz] * GROUP, GROUP), GROUP)], relay.at[pl.ds(i * GROUP, GROUP)],
-            relay_s.at[i], relay_r.at[i], line[dz],
-        )
-        for i, dz in enumerate(RELAYS)
-    ]
-
     pl.semaphore_wait(ready.at[0], 2)
     for to in x_line:
         pl.semaphore_signal(ready.at[1], inc=1, device_id=(rep, to), device_id_type=MESH)
     for dz in Z_ORDER[:-1]:
         push(code_s.at[z_at[dz] // 2], code_r.at[my_y, my_x, my_z], code_ss.at[0], code_rs.at[0], line[dz])
+
+    pack(*(dz for dz in range(NZ) if dz not in RELAYS))
 
     def hand_on(i):
         blocks[i].wait()

time: 44.8 us -> 44.9 us (level)
  no operation moved by 1% of the time
where the time goes in v6:
time: 44.9 us; the launch traced here: 44.8 us
  Pallas kernels  44.3 us (99%)
  local copies, waits for them, and re-layouts  0.56 us (1%)
    pallas_call x1, Pallas kernels, body(): pl.pallas_call(kernel, out_shape=jax.ShapeDtypeStruct((1, ROWS), jnp.floa...  44.3 us

profile of v6, /device:TPU:1, one launch (start us, length us, event | category | flops | bytes accessed | tf_op | source)
XLA Modules:
  0.0 44.8 jit_solution(2417955980336879421)
XLA Ops:
  0.0 44.3 %shard_map.37 = f32[1,256]{1,0:T(1,128)S(1)} custom-call(bf16[256,1024]{1,0:T(8,128)(2,1)} %emb.1, s32[1,256]{1,0:T(1,128)} %bitcast.4, s32[1,256]{1,0:T(1,128)} %bitcast.5), custom_call_target="tpu_custom_call" | custom-call | tf_op jit(solution)/shard_map/pallas_call | solution.py:296
  44.3 0.6 %copy.5 = f32[256]{0:T(256)} copy(f32[256]{0:T(256)S(1)} %bitcast.3) | data formatting | bytes 2048

commit v7 on v5

--- a/solution.py
+++ b/solution.py
@@ -257,8 +257,6 @@
         for to in peers(dz):
             push(chunk, res_r.at[me], res_ss, res_rs, to)
     res_r[me] = res_s[my_z // 2]
-    landed(send, (OWN - 1 - len(RELAYS)) * MSG, pay_s)
-    landed(res_r, OWN - 1, res_ss)
     landed(res_r, OWN - 1, res_rs)
 
     home = res_r[...].reshape(OWN, 128)
@@ -269,6 +267,8 @@
         value = jnp.sum(jnp.where(lane == base + s, home, 0.0), axis=1, keepdims=True)
         nearest = jnp.where(owner_here & (slot_row == s), value, nearest)
     out_ref[...] = jnp.sum(nearest, axis=0, keepdims=True)
+    landed(send, (OWN - 1 - len(RELAYS)) * MSG, pay_s)
+    landed(res_r, OWN - 1, res_ss)
 
 
 def body(embeddings, cluster, order):

time: 44.8 us -> 44.8 us (level)
  no operation moved by 1% of the time
where the time goes in v7:
time: 44.8 us; the launch traced here: 44.7 us
  Pallas kernels  44.1 us (98%)
  local copies, waits for them, and re-layouts  0.56 us (1%)
    pallas_call x1, Pallas kernels, body(): pl.pallas_call(kernel, out_shape=jax.ShapeDtypeStruct((1, ROWS), jnp.floa...  44.1 us

profile of v7, /device:TPU:1, one launch (start us, length us, event | category | flops | bytes accessed | tf_op | source)
XLA Modules:
  0.0 44.7 jit_solution(12605339168339206081)
XLA Ops:
  0.0 44.1 %shard_map.37 = f32[1,256]{1,0:T(1,128)S(1)} custom-call(bf16[256,1024]{1,0:T(8,128)(2,1)} %emb.1, s32[1,256]{1,0:T(1,128)} %bitcast.4, s32[1,256]{1,0:T(1,128)} %bitcast.5), custom_call_target="tpu_custom_call" | custom-call | tf_op jit(solution)/shard_map/pallas_call | solution.py:282
  44.1 0.6 %copy.5 = f32[256]{0:T(256)} copy(f32[256]{0:T(256)S(1)} %bitcast.3) | data formatting | bytes 2048
